TPU v7x, 256 devices: a whole 4x4x8 slice. The times are simulated.
256 devices in a mesh: row: 16 (over y, x), col: 8 (over z), vox: 2 (over core).
Axes of the slice: x: 4, y: 4, z: 8, core: 2. Of those that a mesh axis runs over, the one named last changes fastest.
Arguments:
- coeffs_r: bfloat16 [32, 16, 64, 2, 1024], P(None, 'row', None, None, 'col'), may hold values from -0.125 to 0.125
- rhs: bfloat16 [32, 16, 64, 1536], P('col', 'row', None, 'vox'), may hold values from -6 to 6
- inverses: bfloat16 [2, 1024, 1024], replicated, may hold values from -0.1875 to 0.1875
Outputs:
- updated: bfloat16 [32, 16, 64, 1536], P('col', 'row', None, 'vox')
All inputs are finite; a program needn't handle non-finite values.
Results may differ from a plain program's by a relative error of at most 0.0049.
Values may be sent and summed in bfloat16 or wider, within the bound.
A program may use at most 64 MiB of HBM per device.

v0:
```python
import jax
import jax.numpy as jnp
from jax import lax
from jax.sharding import PartitionSpec as P


def spread(value, axis, root):
    mine = lax.axis_index(axis) == root
    return lax.psum(jnp.where(mine, value, jnp.zeros_like(value)), axis)


def solve_block(inverse, rhs_block, col_pos, own_cols):
    solved_all = jnp.dot(inverse, rhs_block, preferred_element_type=jnp.float32).astype(
        jnp.bfloat16
    )
    solved_mine = lax.dynamic_slice_in_dim(solved_all, col_pos * own_cols, own_cols, 0)
    return (solved_all, solved_mine)


def local(coeffs_r, rhs, inverses):
    row_count = lax.axis_size("row")
    col_count = lax.axis_size("col")
    row_pos = lax.axis_index("row")
    col_pos = lax.axis_index("col")
    per_col = rhs.shape[0]
    block_rows = rhs.shape[2]
    voxels = rhs.shape[3]
    cycles = coeffs_r.shape[0]
    own_cols = coeffs_r.shape[4]
    block_order = inverses.shape[1]
    tail_cycles = block_order // (block_rows * row_count)
    owner_col = col_count - 1
    tail_piece = rhs[per_col - tail_cycles :]
    tail_rows = lax.all_gather(tail_piece, "row", axis=1, tiled=True)
    tail_rows = spread(tail_rows, "col", owner_col)
    solved_last, last_mine = solve_block(
        inverses[1], tail_rows.reshape(block_order, voxels), col_pos, own_cols
    )
    panel_rows = coeffs_r[cycles - 2 * tail_cycles : cycles - tail_cycles, 0, :, 1, :]
    panel_rows = panel_rows.reshape(tail_cycles * block_rows, own_cols)
    partial_value = -jnp.dot(panel_rows, last_mine, preferred_element_type=jnp.float32)
    known = rhs[per_col - 2 * tail_cycles : per_col - tail_cycles, 0]
    known = known.reshape(tail_cycles * block_rows, voxels).astype(jnp.float32)
    partial_value = partial_value + jnp.where(col_pos == owner_col, known, jnp.zeros_like(known))
    partial_value = partial_value.reshape(tail_cycles, 1, block_rows, voxels)
    padded = jnp.zeros((tail_cycles, row_count, block_rows, voxels), jnp.float32)
    anchor = jnp.zeros((), jnp.int32)
    padded = lax.dynamic_update_slice(padded, partial_value, (anchor, row_pos, anchor, anchor))
    middle_rhs = lax.psum(padded, ("row", "col")).astype(jnp.bfloat16)
    solved_first, first_mine = solve_block(
        inverses[0], middle_rhs.reshape(block_order, voxels), col_pos, own_cols
    )
    stacked_mine = jnp.stack([first_mine, last_mine])
    removed = lax.psum_scatter(
        jnp.einsum("kprjc,jcv->kprv", coeffs_r, stacked_mine, preferred_element_type=jnp.float32),
        "col",
        scatter_dimension=0,
        tiled=True,
    )
    remaining = (rhs.astype(jnp.float32) - removed).astype(jnp.bfloat16)

    def my_rows(solved):
        shaped = solved.reshape(tail_cycles, row_count, block_rows, voxels)
        return lax.dynamic_slice_in_dim(shaped, row_pos, 1, 1)

    window = jnp.concatenate([my_rows(solved_first), my_rows(solved_last)], 0)
    lower_part = jnp.where(col_pos == owner_col, window, remaining[per_col - 2 * tail_cycles :])
    return jnp.concatenate([remaining[: per_col - 2 * tail_cycles], lower_part], 0)


def solution(mesh):
    placed = (P(None, "row", None, None, "col"), P("col", "row", None, "vox"), P())
    return jax.shard_map(
        local, mesh=mesh, in_specs=placed, out_specs=P("col", "row", None, "vox"), check_vma=False
    )
```

profile of v0, /device:TPU:1, one launch (start us, length us, event | category | flops | bytes accessed | tf_op | source)
XLA Modules:
  0.0 951.8 jit_solution(15609546226498273052)
XLA Ops:
  6.5 0.0 all-gather.2.cloned.1.call-start
  6.5 1.5 slice.28
  8.1 0.0 all-gather.2.cloned.1.call-update
  8.1 0.0 all-reduce.3.cloned.1.call-start
  8.2 53.5 %all-gather.2.cloned.1.call-done = bf16[1,16,64,768]{3,2,0,1:T(8,128)(2,1)} async-done(((bf16[1,1,64,768]{3,2,0,1:T(8,128)(2,1)}), bf16[1,16,64,768]{3,2,0,1:T(8,128)(2,1)}) %all-gather.2.cloned.1.call-update) | async-done | bytes 1572880 | tf_op jit(solution)/shard_map/all_gather | solution.py:34
  61.6 1.3 broadcast_select_fusion
  62.9 0.0 all-reduce.3.cloned.1.call-update
  62.9 0.0 reduce-scatter.2.cloned.1.call-start
  63.0 1.4 slice.23
  64.4 75.1 %all-reduce.3.cloned.1.call-done = bf16[1024,768]{1,0:T(8,128)(2,1)} async-done(((bf16[1024,768]{1,0:T(8,128)(2,1)}), bf16[1024,768]{1,0:T(8,128)(2,1)}) %all-reduce.3.cloned.1.call-update) | async-done | bytes 1572880 | tf_op jit(solution)/shard_map/psum | solution.py:9
  139.5 3.9 fusion.6
  143.4 0.0 copy-start
  143.4 0.8 dynamic-slice_bitcast_fusion.1
  144.3 0.0 copy-start.3
  144.3 0.0 copy-start.5
  144.3 0.3 broadcast_in_dim.9
  144.6 0.0 copy-done
  144.6 0.6 copy-done.3
  145.2 0.0 copy-done.5
  145.2 0.2 fusion.15
  145.5 610.3 %all-reduce.4 = bf16[1,16,64,768]{3,2,1,0:T(8,128)(2,1)} all-reduce(f32[1,16,64,768]{3,2,1,0:T(8,128)S(1)} %fusion.15), channel_id=1, replica_groups=mesh['row'=16,'col'=8,'vox'=2] {'row','col'}, use_global_device_ids=true, to_apply=%region_1.2 | all-reduce | flops 786432 | bytes 4718592 | tf_op jit(solution)/shard_map/psum | solution.py:49
  755.8 0.0 copy-start.2
  755.8 0.0 copy-start.4
  755.8 4.0 fusion.9
  759.8 0.1 dynamic-slice_bitcast_fusion
  759.9 0.0 copy-done.2
  759.9 0.0 copy-done.4
  759.9 3.7 convolution_bitcast_fusion
  763.6 0.0 copy-start.1
  763.6 0.0 reduce-scatter.2.cloned.1.call-update
  763.6 1.4 copy-done.1
  765.0 1.6 copy.26
  766.5 0.7 copy.24
  767.2 0.9 constant_dynamic-slice_fusion
  768.1 175.1 %reduce-scatter.2.cloned.1.call-done = f32[4,1,64,768]{3,2,0,1:T(8,128)} async-done(((f32[32,1,64,768]{3,2,0,1:T(8,128)}), f32[4,1,64,768]{3,2,0,1:T(8,128)}) %reduce-scatter.2.cloned.1.call-update) | async-done | bytes 786448 | tf_op jit(solution)/shard_map/reduce_scatter | solution.py:54
  943.3 1.2 subtract_convert_fusion
  944.5 0.8 maximum_bitcast_fusion.2
  (2 shorter events, 0.0 us)
Async XLA Ops:
  6.5 55.1 %all-gather.2.cloned.1.call-start = ((), (), s32[]{:S(2)}) async-start(), calls=%async_computation.1 | async-start | bytes 1671168 | tf_op jit(solution)/shard_map/all_gather | solution.py:34
  8.1 131.4 %all-reduce.3.cloned.1.call-start = ((), (), s32[]{:S(2)}) async-start(), calls=%async_computation.2 | async-start | bytes 3145728 | tf_op jit(solution)/shard_map/psum | solution.py:9
  62.9 880.4 %reduce-scatter.2.cloned.1.call-start = ((), (), s32[]{:S(2)}) async-start(), calls=%async_computation.3 | async-start | bytes 7077888 | tf_op jit(solution)/shard_map/reduce_scatter | solution.py:54
  143.4 1.2 copy-start
  144.3 1.0 copy-start.3
  144.3 1.0 copy-start.5
  755.8 4.1 copy-start.2
  755.8 4.1 copy-start.4
  763.6 1.4 copy-start.1
Sparse Core Ops, SparseCore 0:
  9.8 51.8 all-gather.1
  64.0 75.4 all-reduce.2
  763.7 179.5 reduce-scatter.1
where the time goes:
time: 952 us
  blocking collectives  610 us (64%)
  waiting for transfers between devices  304 us (32%)
  between operations  13.2 us (1%)
  matrix products  11.8 us (1%)
    psum x1, blocking collectives, local(): middle_rhs = lax.psum(padded, ('row', 'col')).astype(jnp.bfloat16)  610 us
    reduce_scatter x1, waiting for transfers between devices, local(): lax.psum_scatter(jnp.einsum('kprjc,jcv->kprv', coeffs_r, stacked_mine, pr...  175 us
    psum x1, waiting for transfers between devices, spread(): return lax.psum(jnp.where(mine, value, jnp.zeros_like(value)), axis)  75.1 us
    all_gather x1, waiting for transfers between devices, local(): tail_rows = lax.all_gather(tail_piece, 'row', axis=1, tiled=True)  53.5 us
  transfers between devices with their start and end apart: 3, of which 3 were waited for; matrix products, arithmetic and copies ran while one was open for 0% of the time, Pallas kernels for 0%

commit v1 on v0

--- a/solution.py
+++ b/solution.py
@@ -46,7 +46,7 @@
     padded = jnp.zeros((tail_cycles, row_count, block_rows, voxels), jnp.float32)
     anchor = jnp.zeros((), jnp.int32)
     padded = lax.dynamic_update_slice(padded, partial_value, (anchor, row_pos, anchor, anchor))
-    middle_rhs = lax.psum(padded, ("row", "col")).astype(jnp.bfloat16)
+    middle_rhs = lax.psum(lax.psum(padded, "col"), "row").astype(jnp.bfloat16)
     solved_first, first_mine = solve_block(
         inverses[0], middle_rhs.reshape(block_order, voxels), col_pos, own_cols
     )

time: 952 us -> 424 us (0.45)
  blocking collectives: 610 us -> 86.1 us
    psum x1, blocking collectives: 610 us -> 86.1 us  [local(): middle_rhs = lax.psum(lax.psum(padded, 'col'), 'row').astype(jnp.bfloat16)]
    reduce_scatter x1, waiting for transfers between devices: 175 us -> 75.5 us  [local(): lax.psum_scatter(jnp.einsum('kprjc,jcv->kprv', coeffs_r, stacked_mine, pr...]
    psum x0 -> x1, waiting for transfers between devices: none -> 92.4 us  [local(): middle_rhs = lax.psum(lax.psum(padded, 'col'), 'row').astype(jnp.bfloat16)]
  transfers between devices with their start and end apart: 3 -> 4, of which waited for: 3 -> 4; matrix products, arithmetic and copies ran while one was open for 0% -> 2% of each run, Pallas kernels for 0% -> 0%
where the time goes in v1:
time: 424 us; the launch traced here: 423 us
  waiting for transfers between devices  297 us (70%)
  blocking collectives  86.1 us (20%)
  between operations  13.3 us (3%)
  local copies, waits for them, and re-layouts  12.8 us (3%)
  matrix products  11.3 us (3%)
    psum x1, waiting for transfers between devices, local(): middle_rhs = lax.psum(lax.psum(padded, 'col'), 'row').astype(jnp.bfloat16)  92.4 us
    psum x1, blocking collectives, local(): middle_rhs = lax.psum(lax.psum(padded, 'col'), 'row').astype(jnp.bfloat16)  86.1 us
    reduce_scatter x1, waiting for transfers between devices, local(): lax.psum_scatter(jnp.einsum('kprjc,jcv->kprv', coeffs_r, stacked_mine, pr...  75.5 us
    psum x1, waiting for transfers between devices, spread(): return lax.psum(jnp.where(mine, value, jnp.zeros_like(value)), axis)  75.1 us
    all_gather x1, waiting for transfers between devices, local(): tail_rows = lax.all_gather(tail_piece, 'row', axis=1, tiled=True)  53.5 us
  transfers between devices with their start and end apart: 4, of which 4 were waited for; matrix products, arithmetic and copies ran while one was open for 2% of the time, Pallas kernels for 0%

profile of v1, /device:TPU:1, one launch (start us, length us, event | category | flops | bytes accessed | tf_op | source)
XLA Modules:
  0.0 423.4 jit_solution(16092534142462679838)
XLA Ops:
  6.5 0.0 all-gather.2.cloned.1.call-start
  6.5 1.5 slice.28
  8.1 0.0 all-gather.2.cloned.1.call-update
  8.1 0.0 all-reduce.4.cloned.1.call-start
  8.2 53.5 %all-gather.2.cloned.1.call-done = bf16[1,16,64,768]{3,2,0,1:T(8,128)(2,1)} async-done(((bf16[1,1,64,768]{3,2,0,1:T(8,128)(2,1)}), bf16[1,16,64,768]{3,2,0,1:T(8,128)(2,1)}) %all-gather.2.cloned.1.call-update) | async-done | bytes 1572880 | tf_op jit(solution)/shard_map/all_gather | solution.py:34
  61.6 1.3 broadcast_select_fusion
  62.9 0.0 all-reduce.4.cloned.1.call-update
  62.9 0.0 all-reduce.6.cloned.1.call-start
  63.0 1.4 slice.23
  64.4 75.1 %all-reduce.4.cloned.1.call-done = bf16[1024,768]{1,0:T(8,128)(2,1)} async-done(((bf16[1024,768]{1,0:T(8,128)(2,1)}), bf16[1024,768]{1,0:T(8,128)(2,1)}) %all-reduce.4.cloned.1.call-update) | async-done | bytes 1572880 | tf_op jit(solution)/shard_map/psum | solution.py:9
  139.5 3.9 fusion.6
  143.4 0.0 copy-start.1
  143.4 0.0 copy-start.4
  143.4 0.0 copy-start.7
  143.4 0.3 broadcast_in_dim.9
  143.7 0.8 copy-done.1
  144.6 0.1 copy-done.4
  144.7 0.0 copy-done.7
  144.7 0.2 fusion.15
  144.9 0.0 copy-start
  144.9 1.7 copy-done
  146.6 0.0 all-reduce.6.cloned.1.call-update
  146.6 0.0 reduce-scatter.2.cloned.1.call-start
  146.7 1.6 dynamic-slice_bitcast_fusion.1
  148.3 92.4 %all-reduce.6.cloned.1.call-done = f32[1,16,64,768]{3,2,1,0:T(8,128)} async-done(((f32[1,16,64,768]{3,2,1,0:T(8,128)}), f32[1,16,64,768]{3,2,1,0:T(8,128)}) %all-reduce.6.cloned.1.call-update) | async-done | bytes 3145744 | tf_op jit(solution)/shard_map/psum | solution.py:49
  240.7 86.1 %all-reduce.7 = bf16[1,16,64,768]{3,2,1,0:T(8,128)(2,1)S(1)} all-reduce(f32[1,16,64,768]{3,2,1,0:T(8,128)} %all-reduce.6.cloned.1.call-done), channel_id=1, replica_groups=mesh['row'=16,'col'=8,'vox'=2] {'row'}, use_global_device_ids=true, to_apply=%region_2.3 | all-reduce | flops 786432 | bytes 4718592 | tf_op jit(solution)/shard_map/psum | solution.py:49
  326.8 0.0 copy-start.3
  326.8 0.0 copy-start.5
  326.8 3.5 fusion.9
  330.3 0.1 dynamic-slice_bitcast_fusion
  330.4 0.0 copy-done.3
  330.4 0.0 copy-done.5
  330.4 3.7 convolution_bitcast_fusion
  334.1 0.0 copy-start.2
  334.1 0.0 reduce-scatter.2.cloned.1.call-update
  334.1 1.4 copy-done.2
  335.5 1.6 copy.26
  337.1 1.5 constant_dynamic-slice_fusion
  338.6 0.7 copy.24
  339.3 0.0 copy-start.6
  339.4 75.5 %reduce-scatter.2.cloned.1.call-done = f32[4,1,64,768]{3,2,0,1:T(8,128)} async-done(((f32[32,1,64,768]{3,2,0,1:T(8,128)}), f32[4,1,64,768]{3,2,0,1:T(8,128)}) %reduce-scatter.2.cloned.1.call-update) | async-done | bytes 786448 | tf_op jit(solution)/shard_map/reduce_scatter | solution.py:54
  414.9 1.2 subtract_convert_fusion
  416.1 0.0 copy-done.6
  416.1 0.8 maximum_bitcast_fusion.2
  (2 shorter events, 0.1 us)
Async XLA Ops:
  6.5 55.1 %all-gather.2.cloned.1.call-start = ((), (), s32[]{:S(2)}) async-start(), calls=%async_computation.1 | async-start | bytes 1671168 | tf_op jit(solution)/shard_map/all_gather | solution.py:34
  8.1 131.4 %all-reduce.4.cloned.1.call-start = ((), (), s32[]{:S(2)}) async-start(), calls=%async_computation.2 | async-start | bytes 3145728 | tf_op jit(solution)/shard_map/psum | solution.py:9
  62.9 177.8 %all-reduce.6.cloned.1.call-start = ((), (), s32[]{:S(2)}) async-start(), calls=%async_computation.3 | async-start | bytes 6291456 | tf_op jit(solution)/shard_map/psum | solution.py:49
  143.4 1.2 copy-start.1
  143.4 1.3 copy-start.4
  143.4 1.3 copy-start.7
  144.9 1.7 copy-start
  146.6 268.2 %reduce-scatter.2.cloned.1.call-start = ((), (), s32[]{:S(2)}) async-start(), calls=%async_computation.4 | async-start | bytes 7077888 | tf_op jit(solution)/shard_map/reduce_scatter | solution.py:54
  326.8 3.6 copy-start.3
  326.8 3.6 copy-start.5
  334.1 1.4 copy-start.2
  339.3 76.7 %copy-start.6 = (bf16[1,1,64,768]{3,2,0,1:T(8,128)(2,1)S(1)}, bf16[1,1,64,768]{3,2,0,1:T(8,128)(2,1)}, u32[]{:S(2)}) copy-start(bf16[1,1,64,768]{3,2,0,1:T(8,128)(2,1)} %constant_dynamic-slice_fusion) | copy-start | bytes 294916
Sparse Core Ops, SparseCore 0:
  9.8 51.8 all-gather.1
  64.0 75.4 all-reduce.3
  146.7 93.8 all-reduce.5
  334.3 80.5 reduce-scatter.1

commit v2 on v0

--- a/solution.py
+++ b/solution.py
@@ -6,7 +6,7 @@
 
 def spread(value, axis, root):
     mine = lax.axis_index(axis) == root
-    return lax.psum(jnp.where(mine, value, jnp.zeros_like(value)), axis)
+    return jnp.sum(lax.all_gather(jnp.where(mine, value, jnp.zeros_like(value)), axis), axis=0)
 
 
 def solve_block(inverse, rhs_block, col_pos, own_cols):

time: 952 us -> 1010 us (1.061)
  waiting for transfers between devices: 304 us -> 359 us
    all_gather x0 -> x1, waiting for transfers between devices: none -> 133 us  [spread(): lax.all_gather(jnp.where(mine, value, jnp.zeros_like(value)), axis)]
    psum x1 -> x0, waiting for transfers between devices: 75.1 us -> none  [spread(): return lax.psum(jnp.where(mine, value, jnp.zeros_like(value)), axis)]
where the time goes in v2:
time: 1010 us
  blocking collectives  610 us (60%)
  waiting for transfers between devices  359 us (36%)
  between operations  13.2 us (1%)
  matrix products  11.3 us (1%)
  other arithmetic  10.2 us (1%)
    psum x1, blocking collectives, local(): middle_rhs = lax.psum(padded, ('row', 'col')).astype(jnp.bfloat16)  610 us
    reduce_scatter x1, waiting for transfers between devices, local(): lax.psum_scatter(jnp.einsum('kprjc,jcv->kprv', coeffs_r, stacked_mine, pr...  172 us
    all_gather x1, waiting for transfers between devices, spread(): lax.all_gather(jnp.where(mine, value, jnp.zeros_like(value)), axis)  133 us
    all_gather x1, waiting for transfers between devices, local(): tail_rows = lax.all_gather(tail_piece, 'row', axis=1, tiled=True)  53.5 us
  transfers between devices with their start and end apart: 3, of which 3 were waited for; matrix products, arithmetic and copies ran while one was open for 0% of the time, Pallas kernels for 0%

profile of v2, /device:TPU:1, one launch (start us, length us, event | category | flops | bytes accessed | tf_op | source)
XLA Modules:
  0.0 1011.6 jit_solution(4883538999172181858)
XLA Ops:
  6.5 0.0 all-gather.4.cloned.1.call-start
  6.5 1.5 slice.28
  8.1 0.0 all-gather.4.cloned.1.call-update
  8.1 0.0 all-gather.6.cloned.1.call-start
  8.2 53.5 %all-gather.4.cloned.1.call-done = bf16[1,16,64,768]{3,2,0,1:T(8,128)(2,1)} async-done(((bf16[1,1,64,768]{3,2,0,1:T(8,128)(2,1)}), bf16[1,16,64,768]{3,2,0,1:T(8,128)(2,1)}) %all-gather.4.cloned.1.call-update) | async-done | bytes 1572880 | tf_op jit(solution)/shard_map/all_gather | solution.py:34
  61.6 1.3 select_bitcast_fusion
  62.9 0.0 all-gather.6.cloned.1.call-update
  62.9 0.0 reduce-scatter.2.cloned.1.call-start
  63.0 1.4 slice.23
  64.4 132.8 %all-gather.6.cloned.1.call-done = bf16[8,16,64,768]{3,2,1,0:T(8,128)(2,1)} async-done(((bf16[1,16,64,768]{3,2,1,0:T(8,128)(2,1)}), bf16[8,16,64,768]{3,2,1,0:T(8,128)(2,1)}) %all-gather.6.cloned.1.call-update) | async-done | bytes 12582928 | tf_op jit(solution)/shard_map/all_gather | solution.py:9
  197.2 6.9 reduce.2
  204.1 3.4 fusion.6
  207.5 0.0 copy-start
  207.5 0.8 dynamic-slice_bitcast_fusion.1
  208.4 0.0 copy-start.3
  208.4 0.0 copy-start.5
  208.4 0.3 broadcast_in_dim.9
  208.7 0.1 copy-done
  208.8 0.6 copy-done.3
  209.4 0.0 copy-done.5
  209.4 0.2 fusion.15
  209.6 610.0 %all-reduce.1 = bf16[1,16,64,768]{3,2,1,0:T(8,128)(2,1)} all-reduce(f32[1,16,64,768]{3,2,1,0:T(8,128)S(1)} %fusion.15), channel_id=1, replica_groups=mesh['row'=16,'col'=8,'vox'=2] {'row','col'}, use_global_device_ids=true, to_apply=%region_1.2 | all-reduce | flops 786432 | bytes 4718592 | tf_op jit(solution)/shard_map/psum | solution.py:49
  819.6 0.0 copy-start.2
  819.6 0.0 copy-start.4
  819.6 4.0 fusion.9
  823.6 0.1 dynamic-slice_bitcast_fusion
  823.7 0.0 copy-done.2
  823.7 0.0 copy-done.4
  823.7 3.7 convolution_bitcast_fusion
  827.4 0.0 reduce-scatter.2.cloned.1.call-update
  827.4 0.0 copy-start.1
  827.4 1.7 copy.25
  829.1 0.0 copy-done.1
  829.1 0.7 copy.27
  829.8 0.9 constant_dynamic-slice_fusion.1
  830.7 172.3 %reduce-scatter.2.cloned.1.call-done = f32[4,1,64,768]{3,2,0,1:T(8,128)} async-done(((f32[32,1,64,768]{3,2,0,1:T(8,128)}), f32[4,1,64,768]{3,2,0,1:T(8,128)}) %reduce-scatter.2.cloned.1.call-update) | async-done | bytes 786448 | tf_op jit(solution)/shard_map/reduce_scatter | solution.py:54
  1003.0 1.2 subtract_convert_fusion
  1004.3 0.8 maximum_bitcast_fusion.2
  (2 shorter events, 0.0 us)
Async XLA Ops:
  6.5 55.1 %all-gather.4.cloned.1.call-start = ((), (), s32[]{:S(2)}) async-start(), calls=%async_computation.1 | async-start | bytes 1671168 | tf_op jit(solution)/shard_map/all_gather | solution.py:34
  8.1 189.1 %all-gather.6.cloned.1.call-start = ((), (), s32[]{:S(2)}) async-start(), calls=%async_computation.3 | async-start | bytes 14155776 | tf_op jit(solution)/shard_map/all_gather | solution.py:9
  62.9 940.1 %reduce-scatter.2.cloned.1.call-start = ((), (), s32[]{:S(2)}) async-start(), calls=%async_computation.2 | async-start | bytes 7077888 | tf_op jit(solution)/shard_map/reduce_scatter | solution.py:54
  207.5 1.2 copy-start
  208.4 1.0 copy-start.3
  208.4 1.0 copy-start.5
  819.6 4.1 copy-start.2
  819.6 4.1 copy-start.4
  827.4 1.7 copy-start.1
Sparse Core Ops, SparseCore 0:
  9.8 51.8 all-gather.3
  63.4 133.7 all-gather.5
  827.5 175.4 reduce-scatter.1

commit v3 on v0

--- a/solution.py
+++ b/solution.py
@@ -31,7 +31,9 @@
     tail_cycles = block_order // (block_rows * row_count)
     owner_col = col_count - 1
     tail_piece = rhs[per_col - tail_cycles :]
-    tail_rows = lax.all_gather(tail_piece, "row", axis=1, tiled=True)
+    tail_rows = jnp.concatenate(
+        lax.all_to_all(jnp.stack([tail_piece] * lax.axis_size("row")), "row", 0, 0), axis=1
+    )
     tail_rows = spread(tail_rows, "col", owner_col)
     solved_last, last_mine = solve_block(
         inverses[1], tail_rows.reshape(block_order, voxels), col_pos, own_cols

time: 952 us -> 929 us (0.976)
  waiting for transfers between devices: 304 us -> 272 us
    all_gather x1 -> x0, waiting for transfers between devices: 53.5 us -> none  [local(): tail_rows = lax.all_gather(tail_piece, 'row', axis=1, tiled=True)]
    all_to_all x0 -> x1, waiting for transfers between devices: none -> 22.8 us  [local(): lax.all_to_all(jnp.stack([tail_piece] * lax.axis_size('row')), 'row', 0, 0)]
where the time goes in v3:
time: 929 us
  blocking collectives  610 us (66%)
  waiting for transfers between devices  272 us (29%)
  between operations  13.5 us (1%)
  matrix products  11.8 us (1%)
  local copies, waits for them, and re-layouts  10 us (1%)
    psum x1, blocking collectives, local(): middle_rhs = lax.psum(padded, ('row', 'col')).astype(jnp.bfloat16)  610 us
    reduce_scatter x1, waiting for transfers between devices, local(): lax.psum_scatter(jnp.einsum('kprjc,jcv->kprv', coeffs_r, stacked_mine, pr...  175 us
    psum x1, waiting for transfers between devices, spread(): return lax.psum(jnp.where(mine, value, jnp.zeros_like(value)), axis)  74.4 us
    all_to_all x1, waiting for transfers between devices, local(): lax.all_to_all(jnp.stack([tail_piece] * lax.axis_size('row')), 'row', 0, 0)  22.8 us
  transfers between devices with their start and end apart: 3, of which 3 were waited for; matrix products, arithmetic and copies ran while one was open for 0% of the time, Pallas kernels for 0%

profile of v3, /device:TPU:1, one launch (start us, length us, event | category | flops | bytes accessed | tf_op | source)
XLA Modules:
  0.0 929.0 jit_solution(2832155144976847634)
XLA Ops:
  6.5 0.9 slice_bitcast_fusion
  7.4 1.3 stack.8
  8.7 7.6 all-to-all-start
  16.3 0.0 all-reduce.3.cloned.1.call-start
  16.4 22.8 %all-to-all-done = bf16[16,1,1,64,768]{4,3,2,1,0:T(8,128)(2,1)S(1)} async-done(((bf16[16,1,1,64,768]{4,3,2,1,0:T(8,128)(2,1)}), bf16[16,1,1,64,768]{4,3,2,1,0:T(8,128)(2,1)S(1)}, u32[]{:S(2)}, u32[]{:S(2)}) %all-to-all-start) | async-done | bytes 1572896 | tf_op jit(solution)/shard_map/all_to_all | solution.py:35
  39.2 1.3 broadcast_select_fusion
  40.5 0.0 all-reduce.3.cloned.1.call-update
  40.5 0.0 reduce-scatter.2.cloned.1.call-start
  40.6 1.4 slice.26
  42.0 74.4 %all-reduce.3.cloned.1.call-done = bf16[1024,768]{1,0:T(8,128)(2,1)} async-done(((bf16[1024,768]{1,0:T(8,128)(2,1)}), bf16[1024,768]{1,0:T(8,128)(2,1)}) %all-reduce.3.cloned.1.call-update) | async-done | bytes 1572880 | tf_op jit(solution)/shard_map/psum | solution.py:9
  116.4 3.9 fusion.6
  120.3 0.0 copy-start
  120.3 0.8 dynamic-slice_bitcast_fusion.1
  121.1 0.0 copy-start.3
  121.1 0.0 copy-start.5
  121.1 0.3 broadcast_in_dim.9
  121.4 0.1 copy-done
  121.5 0.6 copy-done.3
  122.1 0.0 copy-done.5
  122.1 0.2 fusion.15
  122.3 610.3 %all-reduce.4 = bf16[1,16,64,768]{3,2,1,0:T(8,128)(2,1)} all-reduce(f32[1,16,64,768]{3,2,1,0:T(8,128)S(1)} %fusion.15), channel_id=1, replica_groups=mesh['row'=16,'col'=8,'vox'=2] {'row','col'}, use_global_device_ids=true, to_apply=%region_1.2 | all-reduce | flops 786432 | bytes 4718592 | tf_op jit(solution)/shard_map/psum | solution.py:51
  732.6 0.0 copy-start.2
  732.6 0.0 copy-start.4
  732.6 4.0 fusion.9
  736.6 0.1 dynamic-slice_bitcast_fusion
  736.7 0.0 copy-done.2
  736.7 0.0 copy-done.4
  736.7 3.7 convolution_bitcast_fusion
  740.4 0.0 copy-start.1
  740.4 0.0 reduce-scatter.2.cloned.1.call-update
  740.4 1.4 copy-done.1
  741.8 1.6 copy.16
  743.4 0.7 copy.14
  744.1 0.9 constant_dynamic-slice_fusion
  745.0 175.2 %reduce-scatter.2.cloned.1.call-done = f32[4,1,64,768]{3,2,0,1:T(8,128)} async-done(((f32[32,1,64,768]{3,2,0,1:T(8,128)}), f32[4,1,64,768]{3,2,0,1:T(8,128)}) %reduce-scatter.2.cloned.1.call-update) | async-done | bytes 786448 | tf_op jit(solution)/shard_map/reduce_scatter | solution.py:56
  920.1 1.2 subtract_convert_fusion
  921.4 0.8 maximum_bitcast_fusion.2
  (2 shorter events, 0.0 us)
Async XLA Ops:
  8.7 30.5 %all-to-all-start = ((bf16[16,1,1,64,768]{4,3,2,1,0:T(8,128)(2,1)}), bf16[16,1,1,64,768]{4,3,2,1,0:T(8,128)(2,1)S(1)}, u32[]{:S(2)}, u32[]{:S(2)}) async-start(bf16[16,1,1,64,768]{4,3,2,1,0:T(8,128)(2,1)} %stack.8), calls=%async_computation | async-start | bytes 3145728 | tf_op jit(solution)/shard_map/all_to_all | solution.py:35
  16.3 100.0 %all-reduce.3.cloned.1.call-start = ((), (), s32[]{:S(2)}) async-start(), calls=%async_computation.2 | async-start | bytes 3145728 | tf_op jit(solution)/shard_map/psum | solution.py:9
  40.5 879.6 %reduce-scatter.2.cloned.1.call-start = ((), (), s32[]{:S(2)}) async-start(), calls=%async_computation.3 | async-start | bytes 7077888 | tf_op jit(solution)/shard_map/reduce_scatter | solution.py:56
  120.3 1.2 copy-start
  121.1 1.0 copy-start.3
  121.1 1.0 copy-start.5
  732.6 4.1 copy-start.2
  732.6 4.1 copy-start.4
  740.4 1.4 copy-start.1
Sparse Core Ops, SparseCore 0:
  40.6 75.6 all-reduce.2
  740.6 179.5 reduce-scatter.1
